TPU v7x, 512 devices: a whole 4x8x8 slice. The times are simulated.
512 devices in a mesh: ctx: 32 (over x, y), tp: 16 (over z, core).
Axes of the slice: x: 4, y: 8, z: 8, core: 2. Of those that a mesh axis runs over, the one named last changes fastest.
Arguments:
- prefix_x: bfloat16 [8192, 8192], P('ctx', 'tp'), may hold values from -6 to 6
- prefix_z: bfloat16 [8192, 8192], P('ctx', 'tp'), may hold values from -6 to 6
- prefix_bc: bfloat16 [8192, 256], P(('ctx', 'tp')), may hold values from -6 to 6
- prefix_dt: float32 [128, 8192], P('tp', 'ctx'), may hold values from -6 to 6
- branch_x: bfloat16 [8192, 8192], P('ctx', 'tp'), may hold values from -6 to 6
- branch_z: bfloat16 [8192, 8192], P('ctx', 'tp'), may hold values from -6 to 6
- branch_bc: bfloat16 [8192, 256], P(('ctx', 'tp')), may hold values from -6 to 6
- branch_dt: float32 [128, 8192], P('tp', 'ctx'), may hold values from -6 to 6
- conv_x: bfloat16 [4, 8192], P(None, 'tp'), may hold values from -3 to 3
- conv_bc: bfloat16 [4, 256], replicated, may hold values from -3 to 3
- decay_rate: float32 [128], P('tp'), may hold values from 2.4414063e-05 to 0.03
- skip: float32 [128], P('tp'), may hold values from 0.5 to 1.5
- norm_gain: float32 [8192], P('tp'), may hold values from 0.5 to 1.5
- bound_pos: int32 [8], replicated, may hold values from 0 to 8191
- branch_owner: int32 [64], replicated, may hold values from 0 to 31, as said below
- branch_parent: int32 [64], replicated, may hold values from 0 to 7
- branch_len: int32 [64], replicated, may hold values from 1 to 255, as said below
Outputs:
- prefix_out: bfloat16 [8192, 8192], P('ctx', 'tp')
- branch_out: bfloat16 [8192, 8192], P('ctx', 'tp')
Inputs may be any that keep to these rules, and one draw needn't show every extreme that they name: `branch_owner`: every block index 0 to 31 holds exactly 2 branches. `branch_len`: the branches of one block have lengths that sum to at most 256; in every draw some block's sum is exactly 256, and some branch has exactly 255 rows.
All inputs are finite; a program needn't handle non-finite values.
Results may differ from a plain program's by a relative error of at most 0.0034.
Values may be sent and summed in bfloat16 or wider, within the bound.
No kernel may reach another device: no remote copies, remote signals or barrier semaphores. Data moves between devices by JAX's collectives and lax.ppermute only.
A program may use at most 64 MiB of HBM per device.

v0:
```python
import jax
import jax.numpy as jnp
from jax import lax
from jax.sharding import PartitionSpec as P

BR_PER = 2
EPSILON = 1e-05
SLOTS = 8
BF = jnp.bfloat16
F32 = jnp.float32
HIGH = lax.Precision.HIGHEST


def conv_silu(lagged, weights):
    summed = weights[0].astype(F32)[None, :] * lagged[0].astype(F32)
    for tap in range(1, len(lagged)):
        summed = summed + weights[tap].astype(F32)[None, :] * lagged[tap].astype(F32)
    return jax.nn.silu(summed).astype(BF)


def split_conv(convolved, channels, heads):
    length = convolved.shape[0]
    state = (convolved.shape[1] - channels) // 2
    values = convolved[:, :channels].reshape(length, heads, channels // heads)
    return (values, convolved[:, channels : channels + state], convolved[:, channels + state :])


def decays(raw_steps, rates):
    length = raw_steps.shape[1]
    step = jax.nn.softplus(raw_steps)
    log_decay = -rates[:, None] * step
    index = jnp.arange(length, dtype=jnp.int32)
    upper = (index[:, None] <= index[None, :]).astype(F32)
    return (step, log_decay, jnp.dot(log_decay, upper, precision=HIGH))


def intra(values, b_rows, c_rows, step, cumulative, mask):
    scores = jnp.dot(c_rows, b_rows.T, preferred_element_type=F32)
    exponent = jnp.where(mask[None], cumulative[:, :, None] - cumulative[:, None, :], 0.0)
    mixing = jnp.where(mask[None], scores[None] * jnp.exp(exponent) * step[:, None, :], 0.0)
    return jnp.einsum("hts,shp->thp", mixing.astype(BF), values, preferred_element_type=F32)


def pick(array, positions):
    index = jnp.arange(array.shape[1], dtype=jnp.int32)
    hit = index[None, None, :] == positions[:, None, None]
    return jnp.sum(jnp.where(hit, array[None], 0.0), axis=2)


def local_states(values, b_rows, step, cumulative, positions):
    length = cumulative.shape[1]
    ends = pick(cumulative, positions)
    row = jnp.arange(length, dtype=jnp.int32)
    inside = (row[None, :] <= positions[:, None])[:, None, :]
    exponent = jnp.where(inside, ends[:, :, None] - cumulative[None], 0.0)
    weight = jnp.where(inside, jnp.exp(exponent) * step[None], 0.0)
    weighted = (jnp.transpose(weight, (0, 2, 1))[:, :, :, None] * values[None].astype(F32)).astype(
        BF
    )
    states = jnp.einsum("jshp,sn->jhpn", weighted, b_rows, preferred_element_type=F32)
    return (states, ends)


def from_state(c_rows, state, weight):
    result = jnp.einsum("tn,hpn->thp", c_rows, state, preferred_element_type=F32)
    return result * weight.T[:, :, None]


def parts_of(value, count):
    found = []
    for _ in range(count):
        part = lax.reduce_precision(value, 8, 7)
        found.append(part.astype(BF))
        value = value - part
    return found


def body(
    prefix_x,
    prefix_z,
    prefix_bc,
    prefix_dt,
    branch_x,
    branch_z,
    branch_bc,
    branch_dt,
    conv_x,
    conv_bc,
    decay_rate,
    skip,
    norm_gain,
    bound_pos,
    branch_owner,
    branch_parent,
    branch_len,
):
    n_ctx = lax.axis_size("ctx")
    me = lax.axis_index("ctx")
    length, channels = prefix_x.shape
    heads = decay_rate.shape[0]
    width = prefix_bc.shape[1]
    n_state = width // 2
    bounds = bound_pos.shape[0]
    branches = branch_owner.shape[0]
    weights = jnp.concatenate([conv_x, conv_bc], axis=1)
    taps = weights.shape[0]
    tail = taps - 1
    row_width = channels + width
    gathered = lax.all_gather(
        jnp.concatenate([prefix_bc, branch_bc], axis=1), "tp", axis=0, tiled=True
    )
    joined = jnp.concatenate([prefix_x, gathered[:, :width]], axis=1)
    before = lax.ppermute(joined[length - tail :], "ctx", [(i, i + 1) for i in range(n_ctx - 1)])
    extended = jnp.concatenate([before, joined], axis=0)
    lagged = [extended[tap : tap + length] for tap in range(taps)]
    values, b_rows, c_rows = split_conv(conv_silu(lagged, weights), channels, heads)
    step, _, cumulative = decays(prefix_dt, decay_rate)
    block_of = bound_pos // length
    at = bound_pos - block_of * length
    order = jnp.arange(bounds, dtype=jnp.int32)
    slot_of = jnp.sum(
        ((block_of[:, None] == block_of[None, :]) & (order[None, :] < order[:, None])).astype(
            jnp.int32
        ),
        axis=1,
    )
    border = jnp.arange(branches, dtype=jnp.int32)
    same = branch_owner[:, None] == branch_owner[None, :]
    earlier = same & (border[None, :] < border[:, None])
    rank = jnp.sum(earlier.astype(jnp.int32), axis=1)
    start = jnp.sum(jnp.where(earlier, branch_len[None, :], 0), axis=1)
    place = jnp.arange(n_ctx * BR_PER, dtype=jnp.int32)
    chosen = place[:, None] == (branch_owner * BR_PER + rank)[None, :]
    parent_of = jnp.sum(jnp.where(chosen, branch_parent[None, :], 0), axis=1)
    mine = (me * BR_PER + jnp.arange(BR_PER, dtype=jnp.int32))[:, None] == (
        branch_owner * BR_PER + rank
    )[None, :]
    my_len = jnp.sum(jnp.where(mine, branch_len[None, :], 0), axis=1)
    my_start = jnp.sum(jnp.where(mine, start[None, :], 0), axis=1)
    slot_here = (block_of == me)[None, :] & (
        slot_of[None, :] == jnp.arange(SLOTS, dtype=jnp.int32)[:, None]
    )
    positions = jnp.sum(jnp.where(slot_here, at[None, :] + 1, 0), axis=1) - 1
    positions = jnp.concatenate([jnp.full((1,), length - 1, jnp.int32), positions])
    states, ends = local_states(values, b_rows, step, cumulative, positions)
    slices = states.reshape(SLOTS + 1, n_ctx, -1, n_state)
    rows = slices.shape[2]
    end_hi, end_lo = parts_of(slices[0], 2)
    partial = jnp.transpose(slices[1:].astype(BF), (1, 0, 2, 3)).reshape(
        n_ctx, SLOTS * rows, n_state
    )
    per_head = jnp.repeat(
        jnp.pad(ends.T, ((0, 0), (0, n_state - SLOTS - 1))), n_ctx // heads, axis=0
    )
    logs = jnp.stack(parts_of(per_head, 3), axis=1)
    parent_hit = parent_of[:, None] == order[None, :]
    parent_at = jnp.sum(jnp.where(parent_hit, at[None, :], 0), axis=1)
    parent_block = jnp.sum(jnp.where(parent_hit, block_of[None, :], 0), axis=1)
    wanted = parent_at[:, None] + 1 + jnp.arange(tail, dtype=jnp.int32)[None, :]
    wanted = jnp.where((parent_block == me)[:, None], wanted, -1).reshape(-1)
    picker = (wanted[:, None] == jnp.arange(length + tail, dtype=jnp.int32)[None, :]).astype(BF)
    tails = jnp.dot(picker, extended, preferred_element_type=F32).astype(BF)
    tails = tails.reshape(n_ctx, BR_PER * tail * row_width // n_state, n_state)
    pieces = [end_hi, end_lo, partial, tails, logs]
    sent = jnp.concatenate(pieces, axis=1)
    sent = jnp.pad(sent, ((0, 0), (0, -sent.shape[1] % 16), (0, 0)))
    got = lax.all_to_all(sent, "ctx", 0, 0, tiled=True)
    edges = [0]
    for piece in pieces:
        edges.append(edges[-1] + piece.shape[1])
    end_hi, end_lo, partial, tails, logs = [
        got[:, first:last].astype(F32) for first, last in zip(edges[:-1], edges[1:], strict=True)
    ]
    ends = jnp.sum(logs, axis=1)[:, : SLOTS + 1]
    block = jnp.arange(n_ctx, dtype=jnp.int32)
    totals = jnp.sum(jnp.where(block[None, :] <= block[:, None], ends[:, 0][None, :], 0.0), axis=1)
    gap = (totals - ends[:, 0])[:, None] - totals[None, :]
    earlier_block = block[None, :] < block[:, None]
    carry = jnp.where(earlier_block, jnp.exp(jnp.where(earlier_block, gap, 0.0)), 0.0)
    entering = jnp.dot(carry, (end_hi + end_lo).reshape(n_ctx, -1), precision=HIGH)
    held = block[None, :] == block_of[:, None]
    bound_end = jnp.sum(
        jnp.where(
            held[:, :, None]
            & (slot_of[:, None, None] == jnp.arange(SLOTS, dtype=jnp.int32)[None, None, :]),
            ends[None, :, 1:],
            0.0,
        ),
        axis=(1, 2),
    )
    choose = jnp.where(held, jnp.exp(bound_end)[:, None], 0.0)
    slot_pick = (
        held[:, :, None]
        & (slot_of[:, None, None] == jnp.arange(SLOTS, dtype=jnp.int32)[None, None, :])
    ).reshape(bounds, -1)
    bound_state = jnp.dot(choose, entering, precision=HIGH) + jnp.dot(
        slot_pick.astype(BF),
        partial.astype(BF).reshape(n_ctx * SLOTS, -1),
        preferred_element_type=F32,
    )
    seeds = jnp.dot(parent_hit.astype(F32), bound_state, precision=HIGH).reshape(
        n_ctx, BR_PER * rows, n_state
    )
    back = jnp.concatenate([entering.reshape(n_ctx, rows, n_state), seeds], axis=1).astype(BF)
    back = lax.all_to_all(back, "ctx", 0, 0, tiled=True)
    row = jnp.arange(length, dtype=jnp.int32)
    mixed = intra(values, b_rows, c_rows, step, cumulative, row[None, :] <= row[:, None])
    inside = (row[None, :] >= my_start[:, None]) & (row[None, :] < (my_start + my_len)[:, None])
    live = inside[0] | inside[1]
    segment = jnp.where(inside[0], 0, jnp.where(inside[1], 1, BR_PER))
    offset = row - jnp.sum(jnp.where(inside, my_start[:, None], 0), axis=0)
    tail_rows = jnp.sum(tails, axis=0).astype(BF).reshape(BR_PER * tail, row_width)
    branch_joined = jnp.concatenate([branch_x, gathered[:, width:]], axis=1)
    column = jnp.arange(BR_PER * tail, dtype=jnp.int32)
    lagged = []
    for shift in range(tail, 0, -1):
        shifted = jnp.concatenate(
            [jnp.zeros((shift, row_width), BF), branch_joined[: length - shift]], axis=0
        )
        local = jnp.where((offset >= shift)[:, None], shifted, jnp.zeros_like(shifted))
        picker = (
            (segment[:, None] == (column // tail)[None, :])
            & (offset[:, None] < shift)
            & ((column % tail)[None, :] == tail - shift + offset[:, None])
        ).astype(BF)
        lagged.append(local + jnp.dot(picker, tail_rows, preferred_element_type=F32).astype(BF))
    lagged.append(branch_joined)
    b_values, b_b, b_c = split_conv(conv_silu(lagged, weights), channels, heads)
    b_step, b_log, b_cum = decays(branch_dt, decay_rate)
    mask = (segment[:, None] == segment[None, :]) & live[:, None] & (row[None, :] <= row[:, None])
    b_mixed = intra(b_values, b_b, b_c, b_step, b_cum, mask)
    starts = pick(b_cum - b_log, my_start)
    gap = b_cum - jnp.where(inside[0][None, :], starts[0][:, None], starts[1][:, None])
    seed_weight = jnp.where(live[None, :], jnp.exp(jnp.where(live[None, :], gap, 0.0)), 0.0)
    shape = (heads, channels // heads, n_state)
    mixed = mixed + from_state(c_rows, back[:, :rows].reshape(shape), jnp.exp(cumulative))
    for slot in range(BR_PER):
        seed = back[:, (slot + 1) * rows : (slot + 2) * rows].reshape(shape)
        b_mixed = b_mixed + from_state(
            b_c, seed, jnp.where(inside[slot][None, :], seed_weight, 0.0)
        )

    def gate(mixed, values, z):
        mixed = mixed + skip[None, :, None] * values.astype(F32)
        gated = mixed.reshape(length, -1) * jax.nn.silu(z.astype(F32))
        return (gated, jnp.sum(gated * gated, axis=1))

    gated, squares = gate(mixed, values, prefix_z)
    b_gated, b_squares = gate(b_mixed, b_values, branch_z)
    every = lax.all_gather(jnp.stack([squares, b_squares])[None], "tp", axis=0, tiled=True)
    factor = lax.rsqrt(jnp.sum(every, axis=0) / (channels * lax.axis_size("tp")) + EPSILON)
    prefix_out = (gated * factor[0][:, None] * norm_gain[None, :]).astype(BF)
    branch_out = (b_gated * factor[1][:, None] * norm_gain[None, :]).astype(BF)
    return (prefix_out, jnp.where(live[:, None], branch_out, jnp.zeros_like(branch_out)))


def solution(mesh):
    both = P(("ctx", "tp"), None)
    in_specs = (
        P("ctx", "tp"),
        P("ctx", "tp"),
        both,
        P("tp", "ctx"),
        P("ctx", "tp"),
        P("ctx", "tp"),
        both,
        P("tp", "ctx"),
        P(None, "tp"),
        P(),
        P("tp"),
        P("tp"),
        P("tp"),
        P(),
        P(),
        P(),
        P(),
    )
    out_specs = (P("ctx", "tp"), P("ctx", "tp"))
    return jax.shard_map(body, mesh=mesh, in_specs=in_specs, out_specs=out_specs, check_vma=False)
```

profile of v0, /device:TPU:1, one launch (start us, length us, event | category | flops | bytes accessed | tf_op | source)
XLA Modules:
  0.0 158.5 jit_solution(17156961118969503318)
XLA Ops:
  0.6 0.8 pad_maximum_fusion.3
  1.4 25.2 %all_gather.6 = bf16[256,512]{1,0:T(8,128)(2,1)S(1)} all-gather(bf16[16,512]{1,0:T(8,128)(2,1)S(1)} %pad_maximum_fusion.3), channel_id=1, replica_groups=mesh['ctx'=32,'tp'=16] {'tp'}, dimensions={0}, use_global_device_ids=true | all-gather | bytes 278528 | tf_op jit(solution)/shard_map/all_gather | solution.py:109
  26.6 0.7 fusion.90
  27.3 3.2 %collective-permute-start = (bf16[3,768]{1,0:T(4,128)(2,1)S(1)}, bf16[3,768]{1,0:T(4,128)(2,1)S(1)}, u32[]{:S(2)}, u32[]{:S(2)}) collective-permute-start(bf16[3,768]{1,0:T(4,128)(2,1)S(1)} %fusion.90), channel_id=1, source_target_pairs={{0,16},{16,32},{32,48},{48,64},{64,80},{80,96},{96,112},{112,128},... | collective-permute-start | bytes 13832 | tf_op jit(solution)/shard_map/ppermute | solution.py:113
  30.5 0.7 broadcast_compare_fusion.7
  31.2 0.7 broadcast_add_fusion.4
  32.5 0.7 neg.27
  33.1 1.3 compare_select_fusion.1
  34.4 1.5 bitcast_exponential_fusion
  36.0 0.7 constant_dynamic-update-slice_fusion.1
  36.7 1.4 select_reduce_fusion.2
  38.1 0.7 multiply_add_fusion
  38.8 0.8 select_reduce_fusion.3
  40.1 0.7 constant_dynamic-update-slice_fusion
  40.9 0.7 broadcast_and_fusion
  41.9 0.6 copy.57
  42.5 0.6 copy.58
  43.1 1.0 maximum_maximum_fusion
  44.2 0.5 multiply_convert_fusion.3
  45.0 0.8 fusion
  46.0 0.7 fusion.44
  47.7 3.7 %concatenate.39 = bf16[32,199,128]{2,1,0:T(8,128)(2,1)S(1)} concatenate(bf16[32,16,128]{2,1,0:T(8,128)(2,1)} %get-tuple-element.25, bf16[32,16,128]{2,1,0:T(8,128)(2,1)} %get-tuple-element.24, bf16[32,128,128]{2,1,0:T(8,128)(2,1)S(1)} %bitcast.88, bf16[32,36,128]{2,1,0:T(8,128)(2,1)S(1)} %reshape.471, bf16[32,1,128]{2,1,0:T(2,128)(2,1)S(1)} %copy.56, bf16[32,1,128]{2,1,0:T(2,128)(2,1)} %copy.57, ...), dimensions={1} | concatenate | bytes 3260416 | tf_op jit(solution)/shard_map/concatenate | solution.py:165
  51.4 1.3 pad.12
  52.7 8.9 %all-to-all-start = ((bf16[32,208,128]{2,1,0:T(8,128)(2,1)}), bf16[32,208,128]{2,1,0:T(8,128)(2,1)S(1)}, u32[]{:S(2)}, u32[]{:S(2)}) async-start(bf16[32,208,128]{2,1,0:T(8,128)(2,1)} %pad.12), calls=%async_computation | async-start | bytes 3407872 | tf_op jit(solution)/shard_map/all_to_all | solution.py:167
  61.7 0.7 and.137
  62.7 0.6 and_select_fusion
  63.3 0.6 compare_select_fusion
  64.0 0.6 iota_compare_fusion.5
  64.8 0.8 fusion.41
  65.5 0.8 fusion.42
  66.3 0.8 fusion.40
  67.1 0.6 broadcast_compare_fusion.4
  67.7 0.6 iota_subtract_fusion
  68.3 0.7 fusion.92
  69.0 0.8 and_and_fusion
  69.7 0.9 fusion.59
  70.6 31.0 %all-to-all-done = bf16[32,208,128]{2,1,0:T(8,128)(2,1)S(1)} async-done(((bf16[32,208,128]{2,1,0:T(8,128)(2,1)}), bf16[32,208,128]{2,1,0:T(8,128)(2,1)S(1)}, u32[]{:S(2)}, u32[]{:S(2)}) %all-to-all-start) | async-done | bytes 1703968 | tf_op jit(solution)/shard_map/all_to_all | solution.py:167
  101.7 0.6 slice_reduce_fusion.1
  102.3 0.7 slice.183
  103.0 1.1 slice.184
  104.1 1.5 reshape.475
  105.7 1.4 select_reduce_fusion.5
  107.0 1.4 copy.59
  108.4 0.8 subtract_reduce_fusion
  109.2 0.9 select_reduce_fusion
  110.2 1.1 fusion.46
  111.3 0.7 convert_bitcast_fusion
  112.0 0.9 fusion.99
  112.9 0.9 convolution_add_fusion
  113.8 0.4 convolution_convert_fusion
  114.4 0.9 copy.66
  115.3 0.8 pad_maximum_fusion.2
  116.1 7.5 %all-to-all-start.1 = ((bf16[32,48,128]{2,1,0:T(8,128)(2,1)}), bf16[32,48,128]{2,1,0:T(8,128)(2,1)S(1)}, u32[]{:S(2)}, u32[]{:S(2)}) async-start(bf16[32,48,128]{2,1,0:T(8,128)(2,1)} %pad_maximum_fusion.2), calls=%async_computation.1 | async-start | bytes 786432 | tf_op jit(solution)/shard_map/all_to_all | solution.py:205
  123.7 1.5 fusion.16
  125.2 1.1 fusion.19
  126.4 0.7 multiply_convert_fusion.2
  127.2 0.8 copy.61
  128.0 0.9 fusion.52
  128.9 5.3 %all-to-all-done.1 = bf16[32,48,128]{2,1,0:T(8,128)(2,1)S(1)} async-done(((bf16[32,48,128]{2,1,0:T(8,128)(2,1)}), bf16[32,48,128]{2,1,0:T(8,128)(2,1)S(1)}, u32[]{:S(2)}, u32[]{:S(2)}) %all-to-all-start.1) | async-done | bytes 393248 | tf_op jit(solution)/shard_map/all_to_all | solution.py:205
  134.5 0.8 fusion.6
  136.4 0.8 fusion.7
  137.9 18.7 %all-gather.1 = f32[16,2,256]{2,1,0:T(2,128)S(1)} all-gather(f32[1,2,256]{2,1,0:T(2,128)S(1)} %maximum_bitcast_fusion), channel_id=2, replica_groups=mesh['ctx'=32,'tp'=16] {'tp'}, dimensions={0}, use_global_device_ids=true | all-gather | bytes 34816 | tf_op jit(solution)/shard_map/all_gather | solution.py:250
  156.7 0.9 fusion.45
  157.6 0.9 multiply_convert_fusion.5
  (168 shorter events, 5.8 us)
Async XLA Ops:
  0.6 43.6 %copy-start.1 = (bf16[256,512]{1,0:T(8,128)(2,1)S(1)}, bf16[256,512]{1,0:T(8,128)(2,1)}, u32[]{:S(2)}) copy-start(bf16[256,512]{1,0:T(8,128)(2,1)} %param.17) | copy-start | bytes 786436
  27.3 15.8 %collective-permute-start = (bf16[3,768]{1,0:T(4,128)(2,1)S(1)}, bf16[3,768]{1,0:T(4,128)(2,1)S(1)}, u32[]{:S(2)}, u32[]{:S(2)}) collective-permute-start(bf16[3,768]{1,0:T(4,128)(2,1)S(1)} %fusion.90), channel_id=1, source_target_pairs={{0,16},{16,32},{32,48},{48,64},{64,80},{80,96},{96,112},{112,128},... | collective-permute-start | bytes 13832 | tf_op jit(solution)/shard_map/ppermute | solution.py:113
  31.2 8.6 %copy-start.30 = (s32[8]{0:T(128)}, s32[8]{0:T(128)S(1)}, u32[]{:S(2)}) copy-start(s32[8]{0:T(128)S(1)} %get-tuple-element.16) | copy-start | bytes 100
  32.1 12.1 %copy-start.34 = (pred[8,32]{1,0:T(8,128)(4,1)}, pred[8,32]{1,0:T(8,128)(4,1)S(1)}, u32[]{:S(2)}) copy-start(pred[8,32]{1,0:T(8,128)(4,1)S(1)} %iota_compare_fusion.14) | copy-start | bytes 772
  32.2 12.0 %copy-start.35 = (pred[8,8]{1,0:T(8,128)(4,1)}, pred[8,8]{1,0:T(8,128)(4,1)S(1)}, u32[]{:S(2)}) copy-start(pred[8,8]{1,0:T(8,128)(4,1)S(1)} %iota_compare_fusion.13) | copy-start | bytes 196
  33.1 2.8 %copy-start.51 = (f32[8]{0:T(128)}, f32[8]{0:T(128)S(1)}, u32[]{:S(2)}) copy-start(f32[8]{0:T(128)S(1)} %neg.27) | copy-start | bytes 100
  36.0 8.7 %copy-start.20 = (f32[8,256]{1,0:T(8,128)}, f32[8,256]{1,0:T(8,128)S(1)}, u32[]{:S(2)}) copy-start(f32[8,256]{1,0:T(8,128)S(1)} %get-tuple-element.54) | copy-start | bytes 24580
  38.8 0.8 copy-start.45
  39.5 0.5 copy-start.40
  41.7 3.0 %copy-start.14 = (f32[768]{0:T(1024)}, f32[768]{0:T(1024)S(1)}, u32[]{:S(2)}) copy-start(f32[768]{0:T(1024)S(1)} %get-tuple-element.4) | copy-start | bytes 9220
  41.7 3.0 %copy-start.16 = (f32[768]{0:T(1024)}, f32[768]{0:T(1024)S(1)}, u32[]{:S(2)}) copy-start(f32[768]{0:T(1024)S(1)} %get-tuple-element.5) | copy-start | bytes 9220
  41.7 3.0 %copy-start.24 = (f32[768]{0:T(1024)}, f32[768]{0:T(1024)S(1)}, u32[]{:S(2)}) copy-start(f32[768]{0:T(1024)S(1)} %get-tuple-element.2) | copy-start | bytes 9220
  41.7 3.0 %copy-start.26 = (f32[768]{0:T(1024)}, f32[768]{0:T(1024)S(1)}, u32[]{:S(2)}) copy-start(f32[768]{0:T(1024)S(1)} %get-tuple-element.3) | copy-start | bytes 9220
  44.9 0.9 copy-start.5
  52.7 9.0 %copy-start.11 = (pred[8,32,8]{2,1,0:T(8,128)(4,1)S(1)}, pred[8,32,8]{2,1,0:T(8,128)(4,1)}, u32[]{:S(2)}) copy-start(pred[8,32,8]{2,1,0:T(8,128)(4,1)} %broadcast_and_fusion) | copy-start | bytes 6148
  52.7 9.7 %copy-start.42 = (s32[64]{0:T(128)S(1)}, s32[64]{0:T(128)}, u32[]{:S(2)}) copy-start(s32[64]{0:T(128)} %param.33) | copy-start | bytes 772
  52.7 9.7 %copy-start.43 = (s32[64]{0:T(128)S(1)}, s32[64]{0:T(128)}, u32[]{:S(2)}) copy-start(s32[64]{0:T(128)} %get-tuple-element.11) | copy-start | bytes 772
  52.7 9.7 %copy-start.46 = (s32[64]{0:T(128)S(1)}, s32[64]{0:T(128)}, u32[]{:S(2)}) copy-start(s32[64]{0:T(128)} %copy-done.45) | copy-start | bytes 772
  52.7 10.6 %copy-start.49 = (f32[8,256]{1,0:T(8,128)S(1)}, f32[8,256]{1,0:T(8,128)}, u32[]{:S(2)}) copy-start(f32[8,256]{1,0:T(8,128)} %param.24) | copy-start | bytes 24580
  52.7 10.6 %copy-start.52 = (f32[8]{0:T(128)S(1)}, f32[8]{0:T(128)}, u32[]{:S(2)}) copy-start(f32[8]{0:T(128)} %copy-done.51) | copy-start | bytes 100
  52.7 12.0 %copy-start = (bf16[256,512]{1,0:T(8,128)(2,1)S(1)}, bf16[256,512]{1,0:T(8,128)(2,1)}, u32[]{:S(2)}) copy-start(bf16[256,512]{1,0:T(8,128)(2,1)} %param.21) | copy-start | bytes 786436
  52.7 48.9 %all-to-all-start = ((bf16[32,208,128]{2,1,0:T(8,128)(2,1)}), bf16[32,208,128]{2,1,0:T(8,128)(2,1)S(1)}, u32[]{:S(2)}, u32[]{:S(2)}) async-start(bf16[32,208,128]{2,1,0:T(8,128)(2,1)} %pad.12), calls=%async_computation | async-start | bytes 3407872 | tf_op jit(solution)/shard_map/all_to_all | solution.py:167
  62.7 40.3 %copy-start.36 = (pred[256]{0:T(512)(128)(4,1)}, pred[256]{0:T(512)(128)(4,1)S(1)}, u32[]{:S(2)}) copy-start(pred[256]{0:T(512)(128)(4,1)S(1)} %or.10) | copy-start | bytes 772
  64.0 39.1 %copy-start.32 = (f32[8,256]{1,0:T(8,128)}, f32[8,256]{1,0:T(8,128)S(1)}, u32[]{:S(2)}) copy-start(f32[8,256]{1,0:T(8,128)S(1)} %get-tuple-element.52) | copy-start | bytes 24580
  67.1 35.9 %copy-start.22 = (s32[256]{0:T(256)}, s32[256]{0:T(256)S(1)}, u32[]{:S(2)}) copy-start(s32[256]{0:T(256)S(1)} %select_select_fusion.1) | copy-start | bytes 3076
  108.4 5.4 %copy-start.41 = (s32[64]{0:T(128)S(1)}, s32[64]{0:T(128)}, u32[]{:S(2)}) copy-start(s32[64]{0:T(128)} %copy-done.40) | copy-start | bytes 772
  112.9 10.8 %copy-start.17 = (f32[768]{0:T(1024)S(1)}, f32[768]{0:T(1024)}, u32[]{:S(2)}) copy-start(f32[768]{0:T(1024)} %copy-done.16) | copy-start | bytes 9220
  112.9 10.8 %copy-start.23 = (s32[256]{0:T(256)S(1)}, s32[256]{0:T(256)}, u32[]{:S(2)}) copy-start(s32[256]{0:T(256)} %copy-done.22) | copy-start | bytes 3076
  113.8 11.4 %copy-start.2 = (bf16[255,768]{1,0:T(8,128)(2,1)S(1)}, bf16[255,768]{1,0:T(8,128)(2,1)}, u32[]{:S(2)}) copy-start(bf16[255,768]{1,0:T(8,128)(2,1)} %fusion.42) | copy-start | bytes 1175044
  113.8 11.4 %copy-start.15 = (f32[768]{0:T(1024)S(1)}, f32[768]{0:T(1024)}, u32[]{:S(2)}) copy-start(f32[768]{0:T(1024)} %copy-done.14) | copy-start | bytes 9220
  115.3 11.0 %copy-start.25 = (f32[768]{0:T(1024)S(1)}, f32[768]{0:T(1024)}, u32[]{:S(2)}) copy-start(f32[768]{0:T(1024)} %copy-done.24) | copy-start | bytes 9220
  116.1 10.2 %copy-start.27 = (f32[768]{0:T(1024)S(1)}, f32[768]{0:T(1024)}, u32[]{:S(2)}) copy-start(f32[768]{0:T(1024)} %copy-done.26) | copy-start | bytes 9220
  116.1 10.2 %copy-start.38 = (s32[6]{0:T(128)S(1)}, s32[6]{0:T(128)}, u32[]{:S(2)}) copy-start(s32[6]{0:T(128)} %get-tuple-element.55) | copy-start | bytes 76
  116.1 10.2 %copy-start.39 = (s32[6]{0:T(128)S(1)}, s32[6]{0:T(128)}, u32[]{:S(2)}) copy-start(s32[6]{0:T(128)} %get-tuple-element.56) | copy-start | bytes 76
  116.1 10.2 %copy-start.44 = (s32[256]{0:T(256)S(1)}, s32[256]{0:T(256)}, u32[]{:S(2)}) copy-start(s32[256]{0:T(256)} %get-tuple-element.43) | copy-start | bytes 3076
  116.1 10.2 %copy-start.47 = (pred[256]{0:T(512)(128)(4,1)S(1)}, pred[256]{0:T(512)(128)(4,1)}, u32[]{:S(2)}) copy-start(pred[256]{0:T(512)(128)(4,1)} %get-tuple-element.37) | copy-start | bytes 772
  116.1 10.2 %copy-start.48 = (pred[256]{0:T(512)(128)(4,1)S(1)}, pred[256]{0:T(512)(128)(4,1)}, u32[]{:S(2)}) copy-start(pred[256]{0:T(512)(128)(4,1)} %get-tuple-element.38) | copy-start | bytes 772
  116.1 18.0 %all-to-all-start.1 = ((bf16[32,48,128]{2,1,0:T(8,128)(2,1)}), bf16[32,48,128]{2,1,0:T(8,128)(2,1)S(1)}, u32[]{:S(2)}, u32[]{:S(2)}) async-start(bf16[32,48,128]{2,1,0:T(8,128)(2,1)} %pad_maximum_fusion.2), calls=%async_computation.1 | async-start | bytes 786432 | tf_op jit(solution)/shard_map/all_to_all | solution.py:205
  123.7 2.7 %copy-start.7 = (bf16[253,768]{1,0:T(8,128)(2,1)S(1)}, bf16[253,768]{1,0:T(8,128)(2,1)}, u32[]{:S(2)}) copy-start(bf16[253,768]{1,0:T(8,128)(2,1)} %fusion.40) | copy-start | bytes 1165828
  127.1 7.1 %copy-start.28 = (f32[256,8]{0,1:T(8,128)S(1)}, f32[256,8]{0,1:T(8,128)}, u32[]{:S(2)}) copy-start(f32[256,8]{0,1:T(8,128)} %get-tuple-element.53) | copy-start | bytes 24580
  127.1 7.4 %copy-start.6 = (bf16[256,512]{0,1:T(8,128)(2,1)S(1)}, bf16[256,512]{0,1:T(8,128)(2,1)}, u32[]{:S(2)}) copy-start(bf16[256,512]{0,1:T(8,128)(2,1)} %copy-done.5) | copy-start | bytes 786436
  127.1 7.4 %copy-start.8 = (f32[256,256]{1,0:T(8,128)S(1)}, f32[256,256]{1,0:T(8,128)}, u32[]{:S(2)}) copy-start(f32[256,256]{1,0:T(8,128)} %fusion.59) | copy-start | bytes 786436
  127.1 7.4 %copy-start.12 = (pred[256,256]{1,0:T(8,128)(4,1)S(1)}, pred[256,256]{1,0:T(8,128)(4,1)}, u32[]{:S(2)}) copy-start(pred[256,256]{1,0:T(8,128)(4,1)} %iota_compare_fusion.5) | copy-start | bytes 196612
  127.1 7.4 %copy-start.21 = (f32[8,256]{1,0:T(8,128)S(1)}, f32[8,256]{1,0:T(8,128)}, u32[]{:S(2)}) copy-start(f32[8,256]{1,0:T(8,128)} %copy-done.20) | copy-start | bytes 24580
  127.1 7.4 %copy-start.31 = (f32[8,256]{1,0:T(8,128)S(1)}, f32[8,256]{1,0:T(8,128)}, u32[]{:S(2)}) copy-start(f32[8,256]{1,0:T(8,128)} %get-tuple-element.31) | copy-start | bytes 24580
  127.1 7.4 %copy-start.50 = (f32[8]{0:T(128)S(1)}, f32[8]{0:T(128)}, u32[]{:S(2)}) copy-start(f32[8]{0:T(128)} %param.28) | copy-start | bytes 100
  134.5 1.1 copy-start.19
  134.5 1.3 copy-start.18
  135.3 1.0 copy-start.9
  135.3 1.0 copy-start.10
  135.3 1.0 copy-start.13
  135.3 1.0 copy-start.33
  135.3 1.0 copy-start.53
  136.3 1.0 copy-start.4
  136.3 1.3 copy-start.3
  137.2 19.5 %copy-start.29 = (f32[512]{0:T(512)S(1)}, f32[512]{0:T(512)}, u32[]{:S(2)}) copy-start(f32[512]{0:T(512)} %param.29) | copy-start | bytes 6148
  137.2 19.5 %copy-start.37 = (pred[256]{0:T(512)(128)(4,1)S(1)}, pred[256]{0:T(512)(128)(4,1)}, u32[]{:S(2)}) copy-start(pred[256]{0:T(512)(128)(4,1)} %copy-done.36) | copy-start | bytes 772
where the time goes:
time: 160 us; the launch traced here: 158 us
  blocking collectives  43.9 us (27%)
  waiting for transfers between devices  36.3 us (23%)
  other arithmetic  25.4 us (16%)
  starting transfers between devices  19.6 us (12%)
  local copies, waits for them, and re-layouts  17.9 us (11%)
  matrix products  13.9 us (9%)
    all_to_all x1, waiting for transfers between devices, body(): got = lax.all_to_all(sent, 'ctx', 0, 0, tiled=True)  31 us
    all_gather x1, blocking collectives, body(): lax.all_gather(jnp.concatenate([prefix_bc, branch_bc], axis=1), 'tp', axi...  25.2 us
    all_gather x1, blocking collectives, body(): lax.all_gather(jnp.stack([squares, b_squares])[None], 'tp', axis=0, tiled...  18.7 us
    all_to_all x1, starting transfers between devices, body(): got = lax.all_to_all(sent, 'ctx', 0, 0, tiled=True)  8.92 us
    all_to_all x1, starting transfers between devices, body(): back = lax.all_to_all(back, 'ctx', 0, 0, tiled=True)  7.45 us
    all_to_all x1, waiting for transfers between devices, body(): back = lax.all_to_all(back, 'ctx', 0, 0, tiled=True)  5.25 us
    concatenate x1, local copies, waits for them, and re-layouts, body(): sent = jnp.concatenate(pieces, axis=1)  3.65 us
    dot_general x3, matrix products, body(): jnp.dot(picker, tail_rows, preferred_element_type=F32).astype(BF)  3.24 us
  transfers between devices with their start and end apart: 3, of which 2 were waited for; matrix products, arithmetic and copies ran while one was open for 17% of the time, Pallas kernels for 0%

commit v1 on v0

--- a/solution.py
+++ b/solution.py
@@ -106,9 +106,21 @@
     taps = weights.shape[0]
     tail = taps - 1
     row_width = channels + width
-    gathered = lax.all_gather(
-        jnp.concatenate([prefix_bc, branch_bc], axis=1), "tp", axis=0, tiled=True
-    )
+    x = jnp.concatenate([prefix_bc, branch_bc], axis=1)
+    ways, here, k = (lax.axis_size("tp"), lax.axis_index("tp"), x.shape[0])
+    dims = [n * ways if d == 0 else n for d, n in enumerate(x.shape)]
+    gathered = lax.dynamic_update_slice_in_dim(jnp.zeros(dims, x.dtype), x, here * k, axis=0)
+    going_up = going_down = x
+    for far in range(1, ways // 2 + 1):
+        going_up = lax.ppermute(going_up, "tp", [(d, (d + 1) % ways) for d in range(ways)])
+        gathered = lax.dynamic_update_slice_in_dim(
+            gathered, going_up, (here - far) % ways * k, axis=0
+        )
+        if 2 * far < ways:
+            going_down = lax.ppermute(going_down, "tp", [(d, (d - 1) % ways) for d in range(ways)])
+            gathered = lax.dynamic_update_slice_in_dim(
+                gathered, going_down, (here + far) % ways * k, axis=0
+            )
     joined = jnp.concatenate([prefix_x, gathered[:, :width]], axis=1)
     before = lax.ppermute(joined[length - tail :], "ctx", [(i, i + 1) for i in range(n_ctx - 1)])
     extended = jnp.concatenate([before, joined], axis=0)

time: 160 us -> 170 us (1.062)
  starting transfers between devices: 19.6 us -> 50.4 us
  blocking collectives: 43.9 us -> 25.6 us
  other arithmetic: 25.4 us -> 20.3 us
  waiting for transfers between devices: 36.3 us -> 39.9 us
  local copies, waits for them, and re-layouts: 17.9 us -> 16 us
    ppermute x0 -> x15, starting transfers between devices: none -> 27.7 us  [the longest x7 24.2 us: body(): lax.ppermute(going_down, 'tp', [(d, (d - 1) % ways) for d in range(ways)])]
    all_gather x1 -> x0, blocking collectives: 25.2 us -> none  [body(): lax.all_gather(jnp.concatenate([prefix_bc, branch_bc], axis=1), 'tp', axi...]
    ppermute x0 -> x15, waiting for transfers between devices: none -> 9.16 us  [the longest x8 8.03 us: body(): lax.ppermute(going_up, 'tp', [(d, (d + 1) % ways) for d in range(ways)])]
    all_gather x1, blocking collectives: 18.7 us -> 25.6 us  [body(): lax.all_gather(jnp.stack([squares, b_squares])[None], 'tp', axis=0, tiled...]
    all_to_all x1, waiting for transfers between devices: 31 us -> 25.2 us  [body(): got = lax.all_to_all(sent, 'ctx', 0, 0, tiled=True)]
    all_to_all x1, starting transfers between devices: 8.92 us -> 10.7 us  [body(): got = lax.all_to_all(sent, 'ctx', 0, 0, tiled=True)]
  transfers between devices with their start and end apart: 3 -> 18, of which waited for: 2 -> 15; matrix products, arithmetic and copies ran while one was open for 17% -> 15% of each run, Pallas kernels for 0% -> 0%
where the time goes in v1:
time: 170 us; the launch traced here: 169 us
  starting transfers between devices  50.4 us (30%)
  waiting for transfers between devices  39.9 us (23%)
  blocking collectives  25.6 us (15%)
  other arithmetic  20.3 us (12%)
  local copies, waits for them, and re-layouts  16 us (9%)
  matrix products  15.2 us (9%)
    all_gather x1, blocking collectives, body(): lax.all_gather(jnp.stack([squares, b_squares])[None], 'tp', axis=0, tiled...  25.6 us
    all_to_all x1, waiting for transfers between devices, body(): got = lax.all_to_all(sent, 'ctx', 0, 0, tiled=True)  25.2 us
    ppermute x7, starting transfers between devices, body(): lax.ppermute(going_down, 'tp', [(d, (d - 1) % ways) for d in range(ways)])  24.2 us
    all_to_all x1, starting transfers between devices, body(): got = lax.all_to_all(sent, 'ctx', 0, 0, tiled=True)  10.7 us
    all_to_all x1, starting transfers between devices, body(): back = lax.all_to_all(back, 'ctx', 0, 0, tiled=True)  8.77 us
    ppermute x8, waiting for transfers between devices, body(): lax.ppermute(going_up, 'tp', [(d, (d + 1) % ways) for d in range(ways)])  8.03 us
    all_to_all x1, waiting for transfers between devices, body(): back = lax.all_to_all(back, 'ctx', 0, 0, tiled=True)  5.55 us
    dot_general x3, matrix products, body(): jnp.dot(picker, tail_rows, preferred_element_type=F32).astype(BF)  4.02 us
  transfers between devices with their start and end apart: 18, of which 15 were waited for; matrix products, arithmetic and copies ran while one was open for 15% of the time, Pallas kernels for 0%

profile of v1, /device:TPU:1, one launch (start us, length us, event | category | flops | bytes accessed | tf_op | source)
XLA Modules:
  0.0 168.9 jit_solution(15988136309436710084)
XLA Ops:
  0.6 0.7 constant_dynamic-update-slice_fusion.3
  1.4 0.7 constant_dynamic-update-slice_fusion.2
  2.1 3.5 %collective-permute-start = (bf16[16,512]{1,0:T(8,128)(2,1)S(1)}, bf16[16,512]{1,0:T(8,128)(2,1)S(1)}, u32[]{:S(2)}, u32[]{:S(2)}) collective-permute-start(bf16[16,512]{1,0:T(8,128)(2,1)S(1)} %constant_dynamic-update-slice_fusion.2), channel_id=1, source_target_pairs={{0,1},{1,2},{2,3},{3,4},{4,5},{5,6},{6,7},{7,8},{8,9},{9,10},{10,1... | collective-permute-start | bytes 49160 | tf_op jit(solution)/shard_map/ppermute | solution.py:115
  5.6 3.4 %collective-permute-start.1 = (bf16[16,512]{1,0:T(8,128)(2,1)S(1)}, bf16[16,512]{1,0:T(8,128)(2,1)S(1)}, u32[]{:S(2)}, u32[]{:S(2)}) collective-permute-start(bf16[16,512]{1,0:T(8,128)(2,1)S(1)} %constant_dynamic-update-slice_fusion.2), channel_id=1, source_target_pairs={{0,15},{1,0},{2,1},{3,2},{4,3},{5,4},{6,5},{7,6},{8,7},{9,8},{10,9... | collective-permute-start | bytes 49160 | tf_op jit(solution)/shard_map/ppermute | solution.py:120
  9.0 0.7 broadcast_compare_fusion.7
  9.6 0.7 broadcast_add_fusion.4
  10.5 0.7 constant_dynamic-update-slice_fusion.1
  11.2 1.3 compare_select_fusion.1
  12.6 0.7 neg.27
  13.2 1.5 bitcast_exponential_fusion
  15.1 1.4 select_reduce_fusion.2
  16.5 0.7 multiply_add_fusion
  17.2 0.8 select_reduce_fusion.3
  18.7 0.7 broadcast_and_fusion
  19.5 0.7 constant_dynamic-update-slice_fusion
  20.2 3.1 %collective-permute-start.3 = (bf16[16,512]{1,0:T(8,128)(2,1)S(1)}, bf16[16,512]{1,0:T(8,128)(2,1)S(1)}, u32[]{:S(2)}, u32[]{:S(2)}) collective-permute-start(bf16[16,512]{1,0:T(8,128)(2,1)S(1)} %collective-permute-done.1), channel_id=1, source_target_pairs={{0,15},{1,0},{2,1},{3,2},{4,3},{5,4},{6,5},{7,6},{8,7},{9,8},{10,9... | collective-permute-start | bytes 49160 | tf_op jit(solution)/shard_map/ppermute | solution.py:120
  23.3 0.6 collective-permute-done.2
  24.1 3.5 %collective-permute-start.5 = (bf16[16,512]{1,0:T(8,128)(2,1)S(1)}, bf16[16,512]{1,0:T(8,128)(2,1)S(1)}, u32[]{:S(2)}, u32[]{:S(2)}) collective-permute-start(bf16[16,512]{1,0:T(8,128)(2,1)S(1)} %collective-permute-done.3), channel_id=1, source_target_pairs={{0,15},{1,0},{2,1},{3,2},{4,3},{5,4},{6,5},{7,6},{8,7},{9,8},{10,9... | collective-permute-start | bytes 49160 | tf_op jit(solution)/shard_map/ppermute | solution.py:120
  27.7 0.6 collective-permute-done.4
  28.5 3.5 %collective-permute-start.7 = (bf16[16,512]{1,0:T(8,128)(2,1)S(1)}, bf16[16,512]{1,0:T(8,128)(2,1)S(1)}, u32[]{:S(2)}, u32[]{:S(2)}) collective-permute-start(bf16[16,512]{1,0:T(8,128)(2,1)S(1)} %collective-permute-done.5), channel_id=1, source_target_pairs={{0,15},{1,0},{2,1},{3,2},{4,3},{5,4},{6,5},{7,6},{8,7},{9,8},{10,9... | collective-permute-start | bytes 49160 | tf_op jit(solution)/shard_map/ppermute | solution.py:120
  32.1 0.6 collective-permute-done.6
  32.9 3.5 %collective-permute-start.9 = (bf16[16,512]{1,0:T(8,128)(2,1)S(1)}, bf16[16,512]{1,0:T(8,128)(2,1)S(1)}, u32[]{:S(2)}, u32[]{:S(2)}) collective-permute-start(bf16[16,512]{1,0:T(8,128)(2,1)S(1)} %collective-permute-done.7), channel_id=1, source_target_pairs={{0,15},{1,0},{2,1},{3,2},{4,3},{5,4},{6,5},{7,6},{8,7},{9,8},{10,9... | collective-permute-start | bytes 49160 | tf_op jit(solution)/shard_map/ppermute | solution.py:120
  36.4 0.6 collective-permute-done.8
  37.3 3.5 %collective-permute-start.11 = (bf16[16,512]{1,0:T(8,128)(2,1)S(1)}, bf16[16,512]{1,0:T(8,128)(2,1)S(1)}, u32[]{:S(2)}, u32[]{:S(2)}) collective-permute-start(bf16[16,512]{1,0:T(8,128)(2,1)S(1)} %collective-permute-done.9), channel_id=1, source_target_pairs={{0,15},{1,0},{2,1},{3,2},{4,3},{5,4},{6,5},{7,6},{8,7},{9,8},{10,9... | collective-permute-start | bytes 49160 | tf_op jit(solution)/shard_map/ppermute | solution.py:120
  40.8 0.6 collective-permute-done.10
  41.6 3.5 %collective-permute-start.13 = (bf16[16,512]{1,0:T(8,128)(2,1)S(1)}, bf16[16,512]{1,0:T(8,128)(2,1)S(1)}, u32[]{:S(2)}, u32[]{:S(2)}) collective-permute-start(bf16[16,512]{1,0:T(8,128)(2,1)S(1)} %collective-permute-done.11), channel_id=1, source_target_pairs={{0,15},{1,0},{2,1},{3,2},{4,3},{5,4},{6,5},{7,6},{8,7},{9,8},{10,9... | collective-permute-start | bytes 49160 | tf_op jit(solution)/shard_map/ppermute | solution.py:120
  45.2 0.6 collective-permute-done.12
  46.0 4.2 %collective-permute-done.14 = bf16[16,512]{1,0:T(8,128)(2,1)S(1)} collective-permute-done((bf16[16,512]{1,0:T(8,128)(2,1)S(1)}, bf16[16,512]{1,0:T(8,128)(2,1)S(1)}, u32[]{:S(2)}, u32[]{:S(2)}) %collective-permute-start.14) | collective-permute-done | bytes 16416 | tf_op jit(solution)/shard_map/ppermute | solution.py:115
  50.2 3.2 %collective-permute-start.15 = (bf16[3,768]{1,0:T(4,128)(2,1)S(1)}, bf16[3,768]{1,0:T(4,128)(2,1)S(1)}, u32[]{:S(2)}, u32[]{:S(2)}) collective-permute-start(bf16[3,768]{1,0:T(4,128)(2,1)S(1)} %fusion.90), channel_id=1, source_target_pairs={{0,16},{16,32},{32,48},{48,64},{64,80},{80,96},{96,112},{112,128},... | collective-permute-start | bytes 13832 | tf_op jit(solution)/shard_map/ppermute | solution.py:125
  53.7 0.6 copy.57
  55.8 0.8 fusion
  56.8 0.7 fusion.44
  58.6 3.7 %concatenate.39 = bf16[32,199,128]{2,1,0:T(8,128)(2,1)S(1)} concatenate(bf16[32,16,128]{2,1,0:T(8,128)(2,1)} %get-tuple-element.25, bf16[32,16,128]{2,1,0:T(8,128)(2,1)} %get-tuple-element.24, bf16[32,128,128]{2,1,0:T(8,128)(2,1)S(1)} %bitcast.88, bf16[32,36,128]{2,1,0:T(8,128)(2,1)S(1)} %reshape.471, bf16[32,1,128]{2,1,0:T(2,128)(2,1)S(1)} %copy.56, bf16[32,1,128]{2,1,0:T(2,128)(2,1)} %copy.57, ...), dimensions={1} | concatenate | bytes 3260416 | tf_op jit(solution)/shard_map/concatenate | solution.py:177
  62.2 1.3 pad.12
  63.6 10.7 %all-to-all-start = ((bf16[32,208,128]{2,1,0:T(8,128)(2,1)}), bf16[32,208,128]{2,1,0:T(8,128)(2,1)S(1)}, u32[]{:S(2)}, u32[]{:S(2)}) async-start(bf16[32,208,128]{2,1,0:T(8,128)(2,1)} %pad.12), calls=%async_computation | async-start | bytes 3407872 | tf_op jit(solution)/shard_map/all_to_all | solution.py:179
  74.4 0.7 and.214
  76.0 0.6 compare_select_fusion
  76.7 0.6 iota_compare_fusion.5
  77.5 0.6 broadcast_compare_fusion.4
  78.7 0.7 fusion.92
  79.4 0.8 and_and_fusion
  80.1 0.8 fusion.42
  80.9 0.8 fusion.41
  81.7 0.8 fusion.40
  82.5 0.9 fusion.59
  83.3 25.2 %all-to-all-done = bf16[32,208,128]{2,1,0:T(8,128)(2,1)S(1)} async-done(((bf16[32,208,128]{2,1,0:T(8,128)(2,1)}), bf16[32,208,128]{2,1,0:T(8,128)(2,1)S(1)}, u32[]{:S(2)}, u32[]{:S(2)}) %all-to-all-start) | async-done | bytes 1703968 | tf_op jit(solution)/shard_map/all_to_all | solution.py:179
  109.8 0.7 convert_bitcast_fusion
  110.5 0.9 fusion.99
  111.4 1.1 slice.184
  112.5 1.5 reshape.475
  114.0 1.1 convolution_add_fusion
  115.1 1.1 convolution_convert_fusion
  116.4 0.9 copy.66
  117.3 0.8 pad_maximum_fusion.2
  118.1 8.8 %all-to-all-start.1 = ((bf16[32,48,128]{2,1,0:T(8,128)(2,1)}), bf16[32,48,128]{2,1,0:T(8,128)(2,1)S(1)}, u32[]{:S(2)}, u32[]{:S(2)}) async-start(bf16[32,48,128]{2,1,0:T(8,128)(2,1)} %pad_maximum_fusion.2), calls=%async_computation.1 | async-start | bytes 786432 | tf_op jit(solution)/shard_map/all_to_all | solution.py:217
  127.0 1.5 fusion.19
  128.5 1.1 fusion.16
  129.6 1.4 multiply_convert_fusion.2
  131.4 5.6 %all-to-all-done.1 = bf16[32,48,128]{2,1,0:T(8,128)(2,1)S(1)} async-done(((bf16[32,48,128]{2,1,0:T(8,128)(2,1)}), bf16[32,48,128]{2,1,0:T(8,128)(2,1)S(1)}, u32[]{:S(2)}, u32[]{:S(2)}) %all-to-all-start.1) | async-done | bytes 393248 | tf_op jit(solution)/shard_map/all_to_all | solution.py:217
  137.6 0.8 fusion.7
  138.9 1.8 %fusion.6 = f32[256,8,64]{0,2,1:T(8,128)S(1)} fusion(f32[256,8,64]{0,2,1:T(8,128)S(1)} %convolution_multiply_fusion.2, bf16[256,8,64]{0,2,1:T(8,128)(2,1)S(1)} %bitcast.91, f32[8,256]{1,0:T(8,128)S(1)} %copy-done.26, f32[8,256]{1,0:T(8,128)S(1)} %copy-done.17, f32[256,256]{1,0:T(8,128)} %fusion.59, pred[256,256]{1,0:T(8,128)(4,1)S(1)} %copy-done.9, ...), kind=kOutput, calls=%fused_computation.20 | convolution fusion | flops 70778880 | bytes 1654816 | tf_op jit(solution)/shard_map/hts,shp->thp/dot_general | solution.py:41
  141.4 25.6 %all-gather.1 = f32[16,2,256]{2,1,0:T(2,128)S(1)} all-gather(f32[1,2,256]{2,1,0:T(2,128)S(1)} %maximum_bitcast_fusion), channel_id=2, replica_groups=mesh['ctx'=32,'tp'=16] {'tp'}, dimensions={0}, use_global_device_ids=true | all-gather | bytes 34816 | tf_op jit(solution)/shard_map/all_gather | solution.py:262
  167.0 0.9 multiply_convert_fusion.5
  167.9 0.9 fusion.45
  (197 shorter events, 10.6 us)
Async XLA Ops:
  0.6 49.6 %copy-start.1 = (bf16[256,512]{1,0:T(8,128)(2,1)S(1)}, bf16[256,512]{1,0:T(8,128)(2,1)}, u32[]{:S(2)}) copy-start(bf16[256,512]{1,0:T(8,128)(2,1)} %param.17) | copy-start | bytes 786436
  2.1 18.1 %collective-permute-start = (bf16[16,512]{1,0:T(8,128)(2,1)S(1)}, bf16[16,512]{1,0:T(8,128)(2,1)S(1)}, u32[]{:S(2)}, u32[]{:S(2)}) collective-permute-start(bf16[16,512]{1,0:T(8,128)(2,1)S(1)} %constant_dynamic-update-slice_fusion.2), channel_id=1, source_target_pairs={{0,1},{1,2},{2,3},{3,4},{4,5},{5,6},{6,7},{7,8},{8,9},{9,10},{10,1... | collective-permute-start | bytes 49160 | tf_op jit(solution)/shard_map/ppermute | solution.py:115
  5.6 14.6 %collective-permute-start.1 = (bf16[16,512]{1,0:T(8,128)(2,1)S(1)}, bf16[16,512]{1,0:T(8,128)(2,1)S(1)}, u32[]{:S(2)}, u32[]{:S(2)}) collective-permute-start(bf16[16,512]{1,0:T(8,128)(2,1)S(1)} %constant_dynamic-update-slice_fusion.2), channel_id=1, source_target_pairs={{0,15},{1,0},{2,1},{3,2},{4,3},{5,4},{6,5},{7,6},{8,7},{9,8},{10,9... | collective-permute-start | bytes 49160 | tf_op jit(solution)/shard_map/ppermute | solution.py:120
  9.6 8.6 %copy-start.24 = (s32[8]{0:T(128)}, s32[8]{0:T(128)S(1)}, u32[]{:S(2)}) copy-start(s32[8]{0:T(128)S(1)} %get-tuple-element.16) | copy-start | bytes 100
  10.5 45.0 %copy-start.29 = (pred[8,32]{1,0:T(8,128)(4,1)}, pred[8,32]{1,0:T(8,128)(4,1)S(1)}, u32[]{:S(2)}) copy-start(pred[8,32]{1,0:T(8,128)(4,1)S(1)} %iota_compare_fusion.14) | copy-start | bytes 772
  13.2 1.6 copy-start.42
  14.7 40.8 %copy-start.16 = (f32[8,256]{1,0:T(8,128)}, f32[8,256]{1,0:T(8,128)S(1)}, u32[]{:S(2)}) copy-start(f32[8,256]{1,0:T(8,128)S(1)} %get-tuple-element.54) | copy-start | bytes 24580
  14.8 40.7 %copy-start.31 = (pred[8,8]{1,0:T(8,128)(4,1)}, pred[8,8]{1,0:T(8,128)(4,1)S(1)}, u32[]{:S(2)}) copy-start(pred[8,8]{1,0:T(8,128)(4,1)S(1)} %iota_compare_fusion.13) | copy-start | bytes 196
  17.2 0.8 copy-start.38
  17.9 0.6 copy-start.35
  20.2 3.8 %collective-permute-start.2 = (bf16[16,512]{1,0:T(8,128)(2,1)S(1)}, bf16[16,512]{1,0:T(8,128)(2,1)S(1)}, u32[]{:S(2)}, u32[]{:S(2)}) collective-permute-start(bf16[16,512]{1,0:T(8,128)(2,1)S(1)} %collective-permute-done), channel_id=1, source_target_pairs={{0,1},{1,2},{2,3},{3,4},{4,5},{5,6},{6,7},{7,8},{8,9},{9,10},{10,1... | collective-permute-start | bytes 49160 | tf_op jit(solution)/shard_map/ppermute | solution.py:115
  20.2 4.0 %collective-permute-start.3 = (bf16[16,512]{1,0:T(8,128)(2,1)S(1)}, bf16[16,512]{1,0:T(8,128)(2,1)S(1)}, u32[]{:S(2)}, u32[]{:S(2)}) collective-permute-start(bf16[16,512]{1,0:T(8,128)(2,1)S(1)} %collective-permute-done.1), channel_id=1, source_target_pairs={{0,15},{1,0},{2,1},{3,2},{4,3},{5,4},{6,5},{7,6},{8,7},{9,8},{10,9... | collective-permute-start | bytes 49160 | tf_op jit(solution)/shard_map/ppermute | solution.py:120
  23.9 4.4 %collective-permute-start.4 = (bf16[16,512]{1,0:T(8,128)(2,1)S(1)}, bf16[16,512]{1,0:T(8,128)(2,1)S(1)}, u32[]{:S(2)}, u32[]{:S(2)}) collective-permute-start(bf16[16,512]{1,0:T(8,128)(2,1)S(1)} %collective-permute-done.2), channel_id=1, source_target_pairs={{0,1},{1,2},{2,3},{3,4},{4,5},{5,6},{6,7},{7,8},{8,9},{9,10},{10,1... | collective-permute-start | bytes 49160 | tf_op jit(solution)/shard_map/ppermute | solution.py:115
  24.1 4.4 %collective-permute-start.5 = (bf16[16,512]{1,0:T(8,128)(2,1)S(1)}, bf16[16,512]{1,0:T(8,128)(2,1)S(1)}, u32[]{:S(2)}, u32[]{:S(2)}) collective-permute-start(bf16[16,512]{1,0:T(8,128)(2,1)S(1)} %collective-permute-done.3), channel_id=1, source_target_pairs={{0,15},{1,0},{2,1},{3,2},{4,3},{5,4},{6,5},{7,6},{8,7},{9,8},{10,9... | collective-permute-start | bytes 49160 | tf_op jit(solution)/shard_map/ppermute | solution.py:120
  28.3 4.4 %collective-permute-start.6 = (bf16[16,512]{1,0:T(8,128)(2,1)S(1)}, bf16[16,512]{1,0:T(8,128)(2,1)S(1)}, u32[]{:S(2)}, u32[]{:S(2)}) collective-permute-start(bf16[16,512]{1,0:T(8,128)(2,1)S(1)} %collective-permute-done.4), channel_id=1, source_target_pairs={{0,1},{1,2},{2,3},{3,4},{4,5},{5,6},{6,7},{7,8},{8,9},{9,10},{10,1... | collective-permute-start | bytes 49160 | tf_op jit(solution)/shard_map/ppermute | solution.py:115
  28.5 4.4 %collective-permute-start.7 = (bf16[16,512]{1,0:T(8,128)(2,1)S(1)}, bf16[16,512]{1,0:T(8,128)(2,1)S(1)}, u32[]{:S(2)}, u32[]{:S(2)}) collective-permute-start(bf16[16,512]{1,0:T(8,128)(2,1)S(1)} %collective-permute-done.5), channel_id=1, source_target_pairs={{0,15},{1,0},{2,1},{3,2},{4,3},{5,4},{6,5},{7,6},{8,7},{9,8},{10,9... | collective-permute-start | bytes 49160 | tf_op jit(solution)/shard_map/ppermute | solution.py:120
  32.7 4.4 %collective-permute-start.8 = (bf16[16,512]{1,0:T(8,128)(2,1)S(1)}, bf16[16,512]{1,0:T(8,128)(2,1)S(1)}, u32[]{:S(2)}, u32[]{:S(2)}) collective-permute-start(bf16[16,512]{1,0:T(8,128)(2,1)S(1)} %collective-permute-done.6), channel_id=1, source_target_pairs={{0,1},{1,2},{2,3},{3,4},{4,5},{5,6},{6,7},{7,8},{8,9},{9,10},{10,1... | collective-permute-start | bytes 49160 | tf_op jit(solution)/shard_map/ppermute | solution.py:115
  32.9 4.4 %collective-permute-start.9 = (bf16[16,512]{1,0:T(8,128)(2,1)S(1)}, bf16[16,512]{1,0:T(8,128)(2,1)S(1)}, u32[]{:S(2)}, u32[]{:S(2)}) collective-permute-start(bf16[16,512]{1,0:T(8,128)(2,1)S(1)} %collective-permute-done.7), channel_id=1, source_target_pairs={{0,15},{1,0},{2,1},{3,2},{4,3},{5,4},{6,5},{7,6},{8,7},{9,8},{10,9... | collective-permute-start | bytes 49160 | tf_op jit(solution)/shard_map/ppermute | solution.py:120
  37.1 4.4 %collective-permute-start.10 = (bf16[16,512]{1,0:T(8,128)(2,1)S(1)}, bf16[16,512]{1,0:T(8,128)(2,1)S(1)}, u32[]{:S(2)}, u32[]{:S(2)}) collective-permute-start(bf16[16,512]{1,0:T(8,128)(2,1)S(1)} %collective-permute-done.8), channel_id=1, source_target_pairs={{0,1},{1,2},{2,3},{3,4},{4,5},{5,6},{6,7},{7,8},{8,9},{9,10},{10,1... | collective-permute-start | bytes 49160 | tf_op jit(solution)/shard_map/ppermute | solution.py:115
  37.3 4.4 %collective-permute-start.11 = (bf16[16,512]{1,0:T(8,128)(2,1)S(1)}, bf16[16,512]{1,0:T(8,128)(2,1)S(1)}, u32[]{:S(2)}, u32[]{:S(2)}) collective-permute-start(bf16[16,512]{1,0:T(8,128)(2,1)S(1)} %collective-permute-done.9), channel_id=1, source_target_pairs={{0,15},{1,0},{2,1},{3,2},{4,3},{5,4},{6,5},{7,6},{8,7},{9,8},{10,9... | collective-permute-start | bytes 49160 | tf_op jit(solution)/shard_map/ppermute | solution.py:120
  41.4 4.4 %collective-permute-start.12 = (bf16[16,512]{1,0:T(8,128)(2,1)S(1)}, bf16[16,512]{1,0:T(8,128)(2,1)S(1)}, u32[]{:S(2)}, u32[]{:S(2)}) collective-permute-start(bf16[16,512]{1,0:T(8,128)(2,1)S(1)} %collective-permute-done.10), channel_id=1, source_target_pairs={{0,1},{1,2},{2,3},{3,4},{4,5},{5,6},{6,7},{7,8},{8,9},{9,10},{10,1... | collective-permute-start | bytes 49160 | tf_op jit(solution)/shard_map/ppermute | solution.py:115
  41.6 4.4 %collective-permute-start.13 = (bf16[16,512]{1,0:T(8,128)(2,1)S(1)}, bf16[16,512]{1,0:T(8,128)(2,1)S(1)}, u32[]{:S(2)}, u32[]{:S(2)}) collective-permute-start(bf16[16,512]{1,0:T(8,128)(2,1)S(1)} %collective-permute-done.11), channel_id=1, source_target_pairs={{0,15},{1,0},{2,1},{3,2},{4,3},{5,4},{6,5},{7,6},{8,7},{9,8},{10,9... | collective-permute-start | bytes 49160 | tf_op jit(solution)/shard_map/ppermute | solution.py:120
  45.8 4.4 %collective-permute-start.14 = (bf16[16,512]{1,0:T(8,128)(2,1)S(1)}, bf16[16,512]{1,0:T(8,128)(2,1)S(1)}, u32[]{:S(2)}, u32[]{:S(2)}) collective-permute-start(bf16[16,512]{1,0:T(8,128)(2,1)S(1)} %collective-permute-done.12), channel_id=1, source_target_pairs={{0,1},{1,2},{2,3},{3,4},{4,5},{5,6},{6,7},{7,8},{8,9},{9,10},{10,1... | collective-permute-start | bytes 49160 | tf_op jit(solution)/shard_map/ppermute | solution.py:115
  50.2 4.7 %collective-permute-start.15 = (bf16[3,768]{1,0:T(4,128)(2,1)S(1)}, bf16[3,768]{1,0:T(4,128)(2,1)S(1)}, u32[]{:S(2)}, u32[]{:S(2)}) collective-permute-start(bf16[3,768]{1,0:T(4,128)(2,1)S(1)} %fusion.90), channel_id=1, source_target_pairs={{0,16},{16,32},{32,48},{48,64},{64,80},{80,96},{96,112},{112,128},... | collective-permute-start | bytes 13832 | tf_op jit(solution)/shard_map/ppermute | solution.py:125
  53.5 2.0 %copy-start.11 = (f32[768]{0:T(1024)}, f32[768]{0:T(1024)S(1)}, u32[]{:S(2)}) copy-start(f32[768]{0:T(1024)S(1)} %get-tuple-element.5) | copy-start | bytes 9220
  53.5 2.0 %copy-start.13 = (f32[768]{0:T(1024)}, f32[768]{0:T(1024)S(1)}, u32[]{:S(2)}) copy-start(f32[768]{0:T(1024)S(1)} %get-tuple-element.4) | copy-start | bytes 9220
  53.5 2.0 %copy-start.19 = (f32[768]{0:T(1024)}, f32[768]{0:T(1024)S(1)}, u32[]{:S(2)}) copy-start(f32[768]{0:T(1024)S(1)} %get-tuple-element.2) | copy-start | bytes 9220
  53.5 2.0 %copy-start.20 = (f32[768]{0:T(1024)}, f32[768]{0:T(1024)S(1)}, u32[]{:S(2)}) copy-start(f32[768]{0:T(1024)S(1)} %get-tuple-element.3) | copy-start | bytes 9220
  55.8 0.9 copy-start.5
  63.5 10.8 %copy-start.8 = (pred[8,32,8]{2,1,0:T(8,128)(4,1)S(1)}, pred[8,32,8]{2,1,0:T(8,128)(4,1)}, u32[]{:S(2)}) copy-start(pred[8,32,8]{2,1,0:T(8,128)(4,1)} %broadcast_and_fusion) | copy-start | bytes 6148
  63.5 11.5 %copy-start.36 = (s32[64]{0:T(128)S(1)}, s32[64]{0:T(128)}, u32[]{:S(2)}) copy-start(s32[64]{0:T(128)} %param.33) | copy-start | bytes 772
  63.5 11.5 %copy-start.37 = (s32[64]{0:T(128)S(1)}, s32[64]{0:T(128)}, u32[]{:S(2)}) copy-start(s32[64]{0:T(128)} %get-tuple-element.11) | copy-start | bytes 772
  63.5 11.5 %copy-start.39 = (s32[64]{0:T(128)S(1)}, s32[64]{0:T(128)}, u32[]{:S(2)}) copy-start(s32[64]{0:T(128)} %copy-done.38) | copy-start | bytes 772
  63.5 12.5 %copy-start.40 = (f32[8,256]{1,0:T(8,128)S(1)}, f32[8,256]{1,0:T(8,128)}, u32[]{:S(2)}) copy-start(f32[8,256]{1,0:T(8,128)} %param.24) | copy-start | bytes 24580
  63.6 12.5 %copy-start.43 = (f32[8]{0:T(128)S(1)}, f32[8]{0:T(128)}, u32[]{:S(2)}) copy-start(f32[8]{0:T(128)} %copy-done.42) | copy-start | bytes 100
  63.6 16.6 %copy-start = (bf16[256,512]{1,0:T(8,128)(2,1)S(1)}, bf16[256,512]{1,0:T(8,128)(2,1)}, u32[]{:S(2)}) copy-start(bf16[256,512]{1,0:T(8,128)(2,1)} %param.21) | copy-start | bytes 786436
  63.6 44.9 %all-to-all-start = ((bf16[32,208,128]{2,1,0:T(8,128)(2,1)}), bf16[32,208,128]{2,1,0:T(8,128)(2,1)S(1)}, u32[]{:S(2)}, u32[]{:S(2)}) async-start(bf16[32,208,128]{2,1,0:T(8,128)(2,1)} %pad.12), calls=%async_computation | async-start | bytes 3407872 | tf_op jit(solution)/shard_map/all_to_all | solution.py:179
  74.3 34.8 %copy-start.30 = (pred[8,32]{1,0:T(8,128)(4,1)S(1)}, pred[8,32]{1,0:T(8,128)(4,1)}, u32[]{:S(2)}) copy-start(pred[8,32]{1,0:T(8,128)(4,1)} %copy-done.29) | copy-start | bytes 772
  74.3 34.8 %copy-start.32 = (pred[8,8]{1,0:T(8,128)(4,1)S(1)}, pred[8,8]{1,0:T(8,128)(4,1)}, u32[]{:S(2)}) copy-start(pred[8,8]{1,0:T(8,128)(4,1)} %copy-done.31) | copy-start | bytes 196
  75.4 33.5 %copy-start.33 = (pred[256]{0:T(512)(128)(4,1)}, pred[256]{0:T(512)(128)(4,1)S(1)}, u32[]{:S(2)}) copy-start(pred[256]{0:T(512)(128)(4,1)S(1)} %or.10) | copy-start | bytes 772
  76.7 6.7 %copy-start.27 = (f32[8,256]{1,0:T(8,128)}, f32[8,256]{1,0:T(8,128)S(1)}, u32[]{:S(2)}) copy-start(f32[8,256]{1,0:T(8,128)S(1)} %get-tuple-element.52) | copy-start | bytes 24580
  77.5 33.0 %copy-start.18 = (s32[256]{0:T(256)}, s32[256]{0:T(256)S(1)}, u32[]{:S(2)}) copy-start(s32[256]{0:T(256)S(1)} %select_select_fusion.1) | copy-start | bytes 3076
  80.1 30.3 %copy-start.25 = (s32[8]{0:T(128)S(1)}, s32[8]{0:T(128)}, u32[]{:S(2)}) copy-start(s32[8]{0:T(128)} %copy-done.24) | copy-start | bytes 100
  111.4 2.6 %copy-start.23 = (pred[8,256]{1,0:T(8,128)(4,1)S(1)}, pred[8,256]{1,0:T(8,128)(4,1)}, u32[]{:S(2)}) copy-start(pred[8,256]{1,0:T(8,128)(4,1)} %and.214) | copy-start | bytes 6148
  114.0 13.0 %copy-start.14 = (f32[768]{0:T(1024)S(1)}, f32[768]{0:T(1024)}, u32[]{:S(2)}) copy-start(f32[768]{0:T(1024)} %copy-done.13) | copy-start | bytes 9220
  115.1 13.3 %copy-start.2 = (bf16[254,768]{1,0:T(8,128)(2,1)S(1)}, bf16[254,768]{1,0:T(8,128)(2,1)}, u32[]{:S(2)}) copy-start(bf16[254,768]{1,0:T(8,128)(2,1)} %fusion.41) | copy-start | bytes 1170436
  115.1 13.3 %copy-start.12 = (f32[768]{0:T(1024)S(1)}, f32[768]{0:T(1024)}, u32[]{:S(2)}) copy-start(f32[768]{0:T(1024)} %copy-done.11) | copy-start | bytes 9220
  118.1 18.9 %all-to-all-start.1 = ((bf16[32,48,128]{2,1,0:T(8,128)(2,1)}), bf16[32,48,128]{2,1,0:T(8,128)(2,1)S(1)}, u32[]{:S(2)}, u32[]{:S(2)}) async-start(bf16[32,48,128]{2,1,0:T(8,128)(2,1)} %pad_maximum_fusion.2), calls=%async_computation.1 | async-start | bytes 786432 | tf_op jit(solution)/shard_map/all_to_all | solution.py:217
  126.9 2.7 %copy-start.7 = (bf16[253,768]{1,0:T(8,128)(2,1)S(1)}, bf16[253,768]{1,0:T(8,128)(2,1)}, u32[]{:S(2)}) copy-start(bf16[253,768]{1,0:T(8,128)(2,1)} %fusion.40) | copy-start | bytes 1165828
  131.0 6.0 %copy-start.15 = (f32[256,8]{0,1:T(8,128)S(1)}, f32[256,8]{0,1:T(8,128)}, u32[]{:S(2)}) copy-start(f32[256,8]{0,1:T(8,128)} %get-tuple-element.30) | copy-start | bytes 24580
  131.0 6.4 %copy-start.10 = (pred[256,256]{1,0:T(8,128)(4,1)S(1)}, pred[256,256]{1,0:T(8,128)(4,1)}, u32[]{:S(2)}) copy-start(pred[256,256]{1,0:T(8,128)(4,1)} %and_and_fusion) | copy-start | bytes 196612
  131.0 6.4 %copy-start.28 = (f32[8,256]{1,0:T(8,128)S(1)}, f32[8,256]{1,0:T(8,128)}, u32[]{:S(2)}) copy-start(f32[8,256]{1,0:T(8,128)} %copy-done.27) | copy-start | bytes 24580
  131.1 6.4 %copy-start.41 = (f32[8]{0:T(128)S(1)}, f32[8]{0:T(128)}, u32[]{:S(2)}) copy-start(f32[8]{0:T(128)} %param.28) | copy-start | bytes 100
  131.1 6.4 %copy-start.44 = (f32[8,256]{1,0:T(8,128)S(1)}, f32[8,256]{1,0:T(8,128)}, u32[]{:S(2)}) copy-start(f32[8,256]{1,0:T(8,128)} %get-tuple-element.33) | copy-start | bytes 24580
  137.5 1.1 copy-start.21
  137.5 1.3 copy-start.6
  137.5 1.3 copy-start.9
  137.6 1.3 copy-start.17
  137.6 1.3 copy-start.26
  138.9 2.0 %copy-start.4 = (bf16[256,512]{1,0:T(8,128)(2,1)S(1)}, bf16[256,512]{1,0:T(8,128)(2,1)}, u32[]{:S(2)}) copy-start(bf16[256,512]{1,0:T(8,128)(2,1)} %param.22) | copy-start | bytes 786436
  138.9 2.3 %copy-start.3 = (bf16[256,512]{1,0:T(8,128)(2,1)S(1)}, bf16[256,512]{1,0:T(8,128)(2,1)}, u32[]{:S(2)}) copy-start(bf16[256,512]{1,0:T(8,128)(2,1)} %param.18) | copy-start | bytes 786436
  140.7 26.4 %copy-start.22 = (f32[512]{0:T(512)S(1)}, f32[512]{0:T(512)}, u32[]{:S(2)}) copy-start(f32[512]{0:T(512)} %param.29) | copy-start | bytes 6148
  140.7 27.3 %copy-start.34 = (pred[256]{0:T(512)(128)(4,1)S(1)}, pred[256]{0:T(512)(128)(4,1)}, u32[]{:S(2)}) copy-start(pred[256]{0:T(512)(128)(4,1)} %copy-done.33) | copy-start | bytes 772
